TPU v7x, 128 devices: a whole 4x4x4 slice. The times are simulated.
128 devices in a mesh: user: 8 (over z_hi, x), cand: 8 (over z_lo, y), tensor: 2 (over core).
Axes of the slice: x: 4, y: 4, z: 4 (z_hi: 2, z_lo: 2; z = z_hi * 2 + z_lo), core: 2. Of those that a mesh axis runs over, the one named last changes fastest.
Arguments:
- cand_embed: bfloat16 [8, 4096, 1024], P('user', 'cand'), may hold values from -6 to 6
- cand_ids: int32 [8, 4096], P('user', 'cand'), may hold values from 0 to 255
- hist_ids: int32 [8, 4096], P('user', ('cand', 'tensor')), may hold values from 0 to 255
- hist_len: int32 [8], P('user'), may hold values from 1 to 4096, as said below
- hist_keys: bfloat16 [8, 2, 4096, 1024], P('user', None, ('cand', 'tensor')), may hold values from -6 to 6
- hist_values: bfloat16 [8, 2, 4096, 1024], P('user', None, ('cand', 'tensor')), may hold values from -6 to 6
- w_in: bfloat16 [2, 1024, 4, 1024], P(None, None, None, 'tensor'), may hold values from -0.1875 to 0.1875
- w_out: bfloat16 [2, 1024, 1024], P(None, 'tensor'), may hold values from -0.1875 to 0.1875
Outputs:
- cand_out: float32 [8, 4096, 1024], P('user', 'cand')
Inputs may be any that keep to these rules, and one draw needn't show every extreme that they name: `hist_len`: some user has exactly 4096 live history positions.
All inputs are finite; a program needn't handle non-finite values.
Results may differ from a plain program's by a relative error of at most 0.017.
Values may be sent and summed in bfloat16 or wider, within the bound.
A program may use at most 128 MiB of HBM per device.

v0:
```python
import jax
import jax.numpy as jnp
from jax import lax
from jax.sharding import PartitionSpec as P

HEADS = 8
LAYERS = 2


def row_norm(values):
    return values * lax.rsqrt(jnp.mean(values * values, axis=-1, keepdims=True) + 1e-06)


def on_device(cand_embed, cand_ids, hist_ids, hist_len, hist_keys, hist_values, w_in, w_out):
    tensor_pos = lax.axis_index("tensor")
    width = cand_embed.shape[2]
    local = w_in.shape[3]
    head_dim = width // HEADS
    heads_here = local // head_dim
    scale = head_dim ** (-0.5)
    count = cand_embed.shape[1]
    state = cand_embed[0].astype(jnp.float32)
    cand_item = cand_ids[0]
    length = hist_len[0]
    column = tensor_pos * local
    normed = row_norm(state).astype(jnp.bfloat16)
    for layer in range(LAYERS):
        proj = jax.nn.silu(
            jnp.dot(
                normed, w_in[layer].reshape(width, 4 * local), preferred_element_type=jnp.float32
            )
        )
        proj = proj.reshape(count, 4, local)
        gate_u = proj[:, 0]
        value_b = proj[:, 1].astype(jnp.bfloat16)
        query_b = proj[:, 2].astype(jnp.bfloat16)
        key_b = proj[:, 3].astype(jnp.bfloat16)
        query_h = query_b.reshape(count, heads_here, head_dim).transpose(1, 0, 2)
        empty = jnp.zeros((heads_here, count, head_dim), jnp.float32)
        keys = lax.all_gather(hist_keys[0, layer], ("cand", "tensor"), axis=0, tiled=True)
        values = lax.all_gather(hist_values[0, layer], ("cand", "tensor"), axis=0, tiled=True)
        items = lax.all_gather(hist_ids[0], ("cand", "tensor"), axis=0, tiled=True)
        rows = keys.shape[0]
        keys = lax.dynamic_slice_in_dim(keys, column, local, 1)
        values = lax.dynamic_slice_in_dim(values, column, local, 1)

        def compute(total):
            key_h = keys.reshape(rows, heads_here, head_dim).transpose(1, 0, 2)
            value_h = values.reshape(rows, heads_here, head_dim).transpose(1, 0, 2)
            positions = lax.iota(jnp.int32, rows)
            valid = (positions < length)[None, :] & (items[None, :] != cand_item[:, None])

            def one_head(parts):
                query_one, key_one, value_one = parts
                scores = (
                    jnp.einsum("cd,pd->cp", query_one, key_one, preferred_element_type=jnp.float32)
                    * scale
                )
                weights = jnp.where(valid, jax.nn.silu(scores), 0.0).astype(jnp.bfloat16)
                return jnp.dot(weights, value_one, preferred_element_type=jnp.float32)

            return lax.map(one_head, (query_h, key_h, value_h))

        hist_part = lax.cond(jnp.int32(0) < length, compute, lambda total: total, empty)
        own_scores = (
            jnp.sum(
                query_b.astype(jnp.float32).reshape(count, heads_here, head_dim)
                * key_b.astype(jnp.float32).reshape(count, heads_here, head_dim),
                axis=-1,
            )
            * scale
        )
        own_part = jax.nn.silu(own_scores)[..., None] * value_b.astype(jnp.float32).reshape(
            count, heads_here, head_dim
        )
        attended = (hist_part.transpose(1, 0, 2) + own_part).reshape(count, local)
        product = attended * gate_u
        squares = lax.psum(jnp.sum(product * product, axis=1), "tensor")
        normed_z = (product * lax.rsqrt(squares / width + 1e-06)[:, None]).astype(jnp.bfloat16)
        partial_value = jnp.dot(normed_z, w_out[layer], preferred_element_type=jnp.float32)
        state = state + lax.psum(partial_value.astype(jnp.bfloat16), "tensor").astype(jnp.float32)
        if layer + 1 < LAYERS:
            normed = row_norm(state).astype(jnp.bfloat16)
    return state[None]


def solution(mesh):
    in_specs = (
        P("user", "cand", None),
        P("user", "cand"),
        P("user", ("cand", "tensor")),
        P("user"),
        P("user", None, ("cand", "tensor"), None),
        P("user", None, ("cand", "tensor"), None),
        P(None, None, None, "tensor"),
        P(None, "tensor", None),
    )
    out_specs = P("user", "cand", None)
    return jax.shard_map(
        on_device, mesh=mesh, in_specs=in_specs, out_specs=out_specs, check_vma=False
    )
```

profile of v0, /device:TPU:1, one launch (start us, length us, event | category | flops | bytes accessed | tf_op | source)
XLA Modules:
  0.0 410.3 jit_solution(11231503174238420126)
XLA Ops:
  11.8 7.0 %fusion.62 = (bf16[1,1024,4,512]{3,2,1,0:T(4,128)(2,1)S(1)}, bf16[1,1024,4,512]{3,2,1,0:T(4,128)(2,1)}) fusion(bf16[2,1024,4,512]{3,2,1,0:T(4,128)(2,1)} %param.22), kind=kLoop, calls=%fused_computation.78 | loop fusion | bytes 16777216 | tf_op jit(solution)/shard_map/slice | solution.py:30
  20.5 4.9 %divide_multiply_fusion.1 = f32[512,2048]{1,0:T(8,128)} fusion(bf16[1024,2048]{1,0:T(8,128)(2,1)S(1)} %bitcast.164, bf16[1,512,1024]{2,1,0:T(8,128)(2,1)S(1)} %copy-done, f32[512]{0:T(512)S(1)} %add_rsqrt_fusion.3), kind=kOutput, calls=%fused_computation.37 | convolution fusion | flops 2153250816 | bytes 9439232 | tf_op jit(solution)/shard_map/dot_general | solution.py:29
  25.4 5.4 %copy.25 = f32[512,2048]{0,1:T(8,128)} copy(f32[512,2048]{1,0:T(8,128)} %divide_multiply_fusion.1) | data formatting | bytes 8388608 | tf_op jit(solution)/shard_map/reshape | solution.py:33
  32.1 3.8 convert.15
  36.6 21.6 %all-gather.2 = s32[1,4096]{1,0:T(1,128)S(1)} all-gather(s32[1,256]{1,0:T(1,128)S(1)} %copy-done.5), channel_id=4, replica_groups=mesh['user'=8,'cand'=8,'tensor'=2] {'cand','tensor'}, dimensions={1}, use_global_device_ids=true | all-gather | bytes 17408 | tf_op jit(solution)/shard_map/all_gather | solution.py:42
  60.6 13.5 %all-gather.10.cloned.1.call-done = bf16[1,1,4096,1024]{2,3,1,0:T(8,128)(2,1)} async-done(((bf16[1,1,256,1024]{2,3,1,0:T(8,128)(2,1)}), bf16[1,1,4096,1024]{2,3,1,0:T(8,128)(2,1)}) %all-gather.10.cloned.1.call-update) | async-done | bytes 8388624 | tf_op jit(solution)/shard_map/all_gather | solution.py:40
  74.1 62.4 %all-gather.12.cloned.1.call-done = bf16[1,1,4096,1024]{2,3,1,0:T(8,128)(2,1)} async-done(((bf16[1,1,256,1024]{2,3,1,0:T(8,128)(2,1)}), bf16[1,1,4096,1024]{2,3,1,0:T(8,128)(2,1)}) %all-gather.12.cloned.1.call-update) | async-done | bytes 8388624 | tf_op jit(solution)/shard_map/all_gather | solution.py:41
  136.5 33.8 %conditional.2 = (f32[4,512,128]{2,1,0:T(8,128)}) conditional(s32[]{:T(128)} %convert_element_type.146, () %tuple.33, (bf16[4096,1024]{0,1:T(8,128)(2,1)}, s32[]{:T(128)}, bf16[4096,1024]{0,1:T(8,128)(2,1)}, s32[]{:T(128)}, s32[4096]{0:T(1024)S(1)}, /*index=5*/s32[1,512]{1,0:T(1,128)S(1)}, bf16[4,512,128]{1,2,0:T(8,128)(2,1)S(1)}) %tuple.106), branch_computations={%region_1.2_spmd, %region_2.5_spmd} | conditional | flops 1092620288 | bytes 19296452 | solution.py:64
  136.5 9.4 %constant_dynamic-slice_fusion = (bf16[4096,512]{0,1:T(8,128)(2,1)}, bf16[4096,512]{0,1:T(8,128)(2,1)}) fusion(bf16[4096,1024]{0,1:T(8,128)(2,1)} %get-tuple-element.174, s32[]{:T(128)} %get-tuple-element.170, bf16[4096,1024]{0,1:T(8,128)(2,1)} %get-tuple-element.169), kind=kLoop, calls=%fused_computation.17 | loop fusion | bytes 16777220 | tf_op jit(solution)/shard_map/dynamic_slice | solution.py:45
  146.6 23.7 %while.32 = (s32[]{:T(128)}, f32[4,512,128]{2,1,0:T(8,128)}, bf16[4,512,128]{1,2,0:T(8,128)(2,1)S(1)}, bf16[4,4096,128]{1,2,0:T(8,128)(2,1)}, bf16[4,4096,128]{1...) while((s32[]{:T(128)}, f32[4,512,128]{2,1,0:T(8,128)}, ...), condition=%wide.region_4.4_spmd.clone, body=%wide.region_3.3_spmd.clone.sunk | while | flops 1092616192 | bytes 2515045 | solution.py:62
  146.6 5.9 %fusion.86 = f32[4,512,128]{2,1,0:T(8,128)} fusion(f32[4,512,128]{2,1,0:T(8,128)} %get-tuple-element.446, s32[]{:T(128)S(6)} %copy.49, s32[4096]{0:T(1024)S(1)} %get-tuple-element.460, s32[512]{0:T(512)S(1)} %get-tuple-element.459, pred[4096]{0:T(1024)(128)(4,1)S(1)} %get-tuple-element.461, bf16[4,4096,128]{1,2,0:T(8,128)(2,1)} %get-tuple-element.458, ...), kind=kOutput, calls=%fused_computation.5.clone.1 | convolution fusion | flops 1092616192 | bytes 2514944 | tf_op jit(solution)/shard_map/cond/branch_1_fun/while/body/eval_jaxpr/dot_general | solution.py:60
  152.6 5.9 %fusion.86 = f32[4,512,128]{2,1,0:T(8,128)} fusion(f32[4,512,128]{2,1,0:T(8,128)} %get-tuple-element.446, s32[]{:T(128)S(6)} %copy.49, s32[4096]{0:T(1024)S(1)} %get-tuple-element.460, s32[512]{0:T(512)S(1)} %get-tuple-element.459, pred[4096]{0:T(1024)(128)(4,1)S(1)} %get-tuple-element.461, bf16[4,4096,128]{1,2,0:T(8,128)(2,1)} %get-tuple-element.458, ...), kind=kOutput, calls=%fused_computation.5.clone.1 | convolution fusion | flops 1092616192 | bytes 2514944 | tf_op jit(solution)/shard_map/cond/branch_1_fun/while/body/eval_jaxpr/dot_general | solution.py:60
  158.5 5.9 %fusion.86 = f32[4,512,128]{2,1,0:T(8,128)} fusion(f32[4,512,128]{2,1,0:T(8,128)} %get-tuple-element.446, s32[]{:T(128)S(6)} %copy.49, s32[4096]{0:T(1024)S(1)} %get-tuple-element.460, s32[512]{0:T(512)S(1)} %get-tuple-element.459, pred[4096]{0:T(1024)(128)(4,1)S(1)} %get-tuple-element.461, bf16[4,4096,128]{1,2,0:T(8,128)(2,1)} %get-tuple-element.458, ...), kind=kOutput, calls=%fused_computation.5.clone.1 | convolution fusion | flops 1092616192 | bytes 2514944 | tf_op jit(solution)/shard_map/cond/branch_1_fun/while/body/eval_jaxpr/dot_general | solution.py:60
  164.4 5.9 %fusion.86 = f32[4,512,128]{2,1,0:T(8,128)} fusion(f32[4,512,128]{2,1,0:T(8,128)} %get-tuple-element.446, s32[]{:T(128)S(6)} %copy.49, s32[4096]{0:T(1024)S(1)} %get-tuple-element.460, s32[512]{0:T(512)S(1)} %get-tuple-element.459, pred[4096]{0:T(1024)(128)(4,1)S(1)} %get-tuple-element.461, bf16[4,4096,128]{1,2,0:T(8,128)(2,1)} %get-tuple-element.458, ...), kind=kOutput, calls=%fused_computation.5.clone.1 | convolution fusion | flops 1092616192 | bytes 2514944 | tf_op jit(solution)/shard_map/cond/branch_1_fun/while/body/eval_jaxpr/dot_general | solution.py:60
  173.2 2.5 psum.28
  177.1 3.0 convolution_convert_fusion.1
  182.6 5.6 %copy.38 = bf16[128,8,4,512]{3,1,2,0:T(8,128)(2,1)} copy(bf16[128,8,4,512]{3,2,1,0:T(4,128)(2,1)} %bitcast.149) | data formatting | bytes 8388608
  188.2 17.4 %all-reduce.3.cloned.1.call-done = bf16[512,1024]{1,0:T(8,128)(2,1)} async-done(((bf16[512,1024]{1,0:T(8,128)(2,1)}), bf16[512,1024]{1,0:T(8,128)(2,1)}) %all-reduce.3.cloned.1.call-update) | async-done | bytes 1048592 | tf_op jit(solution)/shard_map/psum | solution.py:81
  207.2 7.3 %divide_multiply_fusion = f32[512,2048]{1,0:T(8,128)} fusion(bf16[1024,2048]{1,0:T(8,128)(2,1)} %bitcast.163, bf16[512,1024]{1,0:T(8,128)(2,1)} %all-reduce.3.cloned.1.call-done, bf16[1,512,1024]{2,1,0:T(8,128)(2,1)S(1)} %copy-done, f32[512]{0:T(512)S(1)} %add_rsqrt_fusion.1), kind=kOutput, calls=%fused_computation.36 | convolution fusion | flops 2154299392 | bytes 10487808 | tf_op jit(solution)/shard_map/dot_general | solution.py:29
  214.5 5.4 %copy.26 = f32[512,2048]{0,1:T(8,128)} copy(f32[512,2048]{1,0:T(8,128)} %divide_multiply_fusion) | data formatting | bytes 8388608 | tf_op jit(solution)/shard_map/reshape | solution.py:33
  224.7 44.4 %all-gather.14.cloned.1.call-done = bf16[1,1,4096,1024]{2,3,1,0:T(8,128)(2,1)} async-done(((bf16[1,1,256,1024]{2,3,1,0:T(8,128)(2,1)}), bf16[1,1,4096,1024]{2,3,1,0:T(8,128)(2,1)}) %all-gather.14.cloned.1.call-update) | async-done | bytes 8388624 | tf_op jit(solution)/shard_map/all_gather | solution.py:40
  269.1 62.2 %all-gather.16.cloned.1.call-done = bf16[1,1,4096,1024]{2,3,1,0:T(8,128)(2,1)} async-done(((bf16[1,1,256,1024]{2,3,1,0:T(8,128)(2,1)}), bf16[1,1,4096,1024]{2,3,1,0:T(8,128)(2,1)}) %all-gather.16.cloned.1.call-update) | async-done | bytes 8388624 | tf_op jit(solution)/shard_map/all_gather | solution.py:41
  331.3 33.8 %conditional.3 = (f32[4,512,128]{2,1,0:T(8,128)}) conditional(s32[]{:T(128)} %convert_element_type.146, () %tuple.35, (bf16[4096,1024]{0,1:T(8,128)(2,1)}, s32[]{:T(128)}, bf16[4096,1024]{0,1:T(8,128)(2,1)}, s32[]{:T(128)}, s32[4096]{0:T(1024)S(1)}, /*index=5*/s32[1,512]{1,0:T(1,128)S(1)}, bf16[4,512,128]{1,2,0:T(8,128)(2,1)S(1)}) %tuple.107), branch_computations={%region_10.11_spmd, %region_11.14_spmd} | conditional | flops 1092620288 | bytes 19296452 | solution.py:64
  331.3 9.4 %constant_dynamic-slice_fusion.2 = (bf16[4096,512]{0,1:T(8,128)(2,1)}, bf16[4096,512]{0,1:T(8,128)(2,1)}) fusion(bf16[4096,1024]{0,1:T(8,128)(2,1)} %get-tuple-element.189, s32[]{:T(128)} %get-tuple-element.185, bf16[4096,1024]{0,1:T(8,128)(2,1)} %get-tuple-element.184), kind=kLoop, calls=%fused_computation.34 | loop fusion | bytes 16777220 | tf_op jit(solution)/shard_map/dynamic_slice | solution.py:45
  341.4 23.7 %while.33 = (s32[]{:T(128)}, f32[4,512,128]{2,1,0:T(8,128)}, bf16[4,512,128]{1,2,0:T(8,128)(2,1)S(1)}, bf16[4,4096,128]{1,2,0:T(8,128)(2,1)}, bf16[4,4096,128]{1...) while((s32[]{:T(128)}, f32[4,512,128]{2,1,0:T(8,128)}, ...), condition=%wide.region_13.13_spmd.clone, body=%wide.region_12.12_spmd.clone.sunk | while | flops 1092616192 | bytes 2515045 | solution.py:62
  341.4 5.9 %fusion.82 = f32[4,512,128]{2,1,0:T(8,128)} fusion(f32[4,512,128]{2,1,0:T(8,128)} %get-tuple-element.419, s32[]{:T(128)S(6)} %copy.42, s32[4096]{0:T(1024)S(1)} %get-tuple-element.433, s32[512]{0:T(512)S(1)} %get-tuple-element.432, pred[4096]{0:T(1024)(128)(4,1)S(1)} %get-tuple-element.434, bf16[4,4096,128]{1,2,0:T(8,128)(2,1)} %get-tuple-element.431, ...), kind=kOutput, calls=%fused_computation.22.clone.1 | convolution fusion | flops 1092616192 | bytes 2514944 | tf_op jit(solution)/shard_map/cond/branch_1_fun/while/body/eval_jaxpr/dot_general | solution.py:60
  347.4 5.9 %fusion.82 = f32[4,512,128]{2,1,0:T(8,128)} fusion(f32[4,512,128]{2,1,0:T(8,128)} %get-tuple-element.419, s32[]{:T(128)S(6)} %copy.42, s32[4096]{0:T(1024)S(1)} %get-tuple-element.433, s32[512]{0:T(512)S(1)} %get-tuple-element.432, pred[4096]{0:T(1024)(128)(4,1)S(1)} %get-tuple-element.434, bf16[4,4096,128]{1,2,0:T(8,128)(2,1)} %get-tuple-element.431, ...), kind=kOutput, calls=%fused_computation.22.clone.1 | convolution fusion | flops 1092616192 | bytes 2514944 | tf_op jit(solution)/shard_map/cond/branch_1_fun/while/body/eval_jaxpr/dot_general | solution.py:60
  353.3 5.9 %fusion.82 = f32[4,512,128]{2,1,0:T(8,128)} fusion(f32[4,512,128]{2,1,0:T(8,128)} %get-tuple-element.419, s32[]{:T(128)S(6)} %copy.42, s32[4096]{0:T(1024)S(1)} %get-tuple-element.433, s32[512]{0:T(512)S(1)} %get-tuple-element.432, pred[4096]{0:T(1024)(128)(4,1)S(1)} %get-tuple-element.434, bf16[4,4096,128]{1,2,0:T(8,128)(2,1)} %get-tuple-element.431, ...), kind=kOutput, calls=%fused_computation.22.clone.1 | convolution fusion | flops 1092616192 | bytes 2514944 | tf_op jit(solution)/shard_map/cond/branch_1_fun/while/body/eval_jaxpr/dot_general | solution.py:60
  359.2 5.9 %fusion.82 = f32[4,512,128]{2,1,0:T(8,128)} fusion(f32[4,512,128]{2,1,0:T(8,128)} %get-tuple-element.419, s32[]{:T(128)S(6)} %copy.42, s32[4096]{0:T(1024)S(1)} %get-tuple-element.433, s32[512]{0:T(512)S(1)} %get-tuple-element.432, pred[4096]{0:T(1024)(128)(4,1)S(1)} %get-tuple-element.434, bf16[4,4096,128]{1,2,0:T(8,128)(2,1)} %get-tuple-element.431, ...), kind=kOutput, calls=%fused_computation.22.clone.1 | convolution fusion | flops 1092616192 | bytes 2514944 | tf_op jit(solution)/shard_map/cond/branch_1_fun/while/body/eval_jaxpr/dot_general | solution.py:60
  371.9 3.0 convolution_convert_fusion
  374.9 25.4 %all-reduce.5.cloned.1.call-done = bf16[512,1024]{1,0:T(8,128)(2,1)} async-done(((bf16[512,1024]{1,0:T(8,128)(2,1)}), bf16[512,1024]{1,0:T(8,128)(2,1)}) %all-reduce.5.cloned.1.call-update) | async-done | bytes 1048592 | tf_op jit(solution)/shard_map/psum | solution.py:81
  400.3 3.1 add_bitcast_fusion
  (59 shorter events, 31.8 us)
Async XLA Ops:
  6.5 3.2 copy-start.4
  6.5 67.6 %all-gather.10.cloned.1.call-start = ((), (), s32[]{:S(2)}) async-start(), calls=%async_computation.2 | async-start | bytes 8912896 | tf_op jit(solution)/shard_map/all_gather | solution.py:40
  9.7 126.8 %all-gather.12.cloned.1.call-start = ((), (), s32[]{:S(2)}) async-start(), calls=%async_computation.3 | async-start | bytes 8912896 | tf_op jit(solution)/shard_map/all_gather | solution.py:41
  11.7 193.8 %all-reduce.3.cloned.1.call-start = ((), (), s32[]{:S(2)}) async-start(), calls=%async_computation | async-start | bytes 2097152 | tf_op jit(solution)/shard_map/psum | solution.py:81
  18.8 1.4 copy-start
  30.7 5.8 %copy-start.5 = (s32[1,256]{1,0:T(1,128)S(1)}, s32[1,256]{1,0:T(1,128)}, u32[]{:S(2)}) copy-start(s32[1,256]{1,0:T(1,128)} %param.18) | copy-start | bytes 3076
  32.1 104.5 %copy-start.6 = (s32[1,512]{1,0:T(1,128)S(1)}, s32[1,512]{1,0:T(1,128)}, u32[]{:S(2)}) copy-start(s32[1,512]{1,0:T(1,128)} %param.17) | copy-start | bytes 6148
  177.1 3.1 copy-start.2
  177.1 4.2 %copy-start.3 = (bf16[1,1,256,1024]{3,2,1,0:T(8,128)(2,1)S(1)}, bf16[1,1,256,1024]{3,2,1,0:T(8,128)(2,1)}, u32[]{:S(2)}) copy-start(bf16[1,1,256,1024]{3,2,1,0:T(8,128)(2,1)} %get-tuple-element.307) | copy-start | bytes 1572868
  180.1 89.0 %all-gather.14.cloned.1.call-start = ((), (), s32[]{:S(2)}) async-start(), calls=%async_computation.4 | async-start | bytes 8912896 | tf_op jit(solution)/shard_map/all_gather | solution.py:40
  181.2 150.1 %all-gather.16.cloned.1.call-start = ((), (), s32[]{:S(2)}) async-start(), calls=%async_computation.5 | async-start | bytes 8912896 | tf_op jit(solution)/shard_map/all_gather | solution.py:41
  182.3 218.0 %all-reduce.5.cloned.1.call-start = ((), (), s32[]{:S(2)}) async-start(), calls=%async_computation.1 | async-start | bytes 2097152 | tf_op jit(solution)/shard_map/psum | solution.py:81
  371.8 28.5 %copy-start.1 = (bf16[512,1024]{1,0:T(8,128)(2,1)S(1)}, bf16[512,1024]{1,0:T(8,128)(2,1)}, u32[]{:S(2)}) copy-start(bf16[512,1024]{1,0:T(8,128)(2,1)} %all-reduce.3.cloned.1.call-done) | copy-start | bytes 3145732
Sparse Core Ops, SparseCore 0:
  9.8 64.2 all-gather.9
  75.7 60.7 all-gather.11
  180.3 25.2 all-reduce.2
  207.1 61.9 all-gather.13
  270.7 60.6 all-gather.15
  375.0 25.2 all-reduce.4
where the time goes:
time: 411 us; the launch traced here: 410 us
  waiting for transfers between devices  225 us (55%)
  matrix products  65.7 us (16%)
  local copies, waits for them, and re-layouts  59.6 us (15%)
  blocking collectives  26.5 us (6%)
  other arithmetic  18.4 us (4%)
  between operations  14.3 us (3%)
    all_gather x2, waiting for transfers between devices, on_device(): lax.all_gather(hist_values[0, layer], ('cand', 'tensor'), axis=0, tiled=T...  125 us
    all_gather x2, waiting for transfers between devices, on_device(): lax.all_gather(hist_keys[0, layer], ('cand', 'tensor'), axis=0, tiled=True)  57.9 us
    dot_general x8, matrix products, one_head(): return jnp.dot(weights, value_one, preferred_element_type=jnp.float32)  47.4 us
    psum x2, waiting for transfers between devices, on_device(): lax.psum(partial_value.astype(jnp.bfloat16), 'tensor').astype(jnp.float32)  42.8 us
    all_gather x1, blocking collectives, on_device(): items = lax.all_gather(hist_ids[0], ('cand', 'tensor'), axis=0, tiled=True)  21.6 us
    dynamic_slice x2, local copies, waits for them, and re-layouts, on_device(): values = lax.dynamic_slice_in_dim(values, column, local, 1)  18.8 us
    dot_general x2, matrix products, on_device(): jnp.dot(normed, w_in[layer].reshape(width, 4 * local), preferred_element_...  12.1 us
    unnamed x20, local copies, waits for them, and re-layouts  11 us
  transfers between devices with their start and end apart: 6, of which 6 were waited for; matrix products, arithmetic and copies ran while one was open for 13% of the time, Pallas kernels for 0%

commit v1 on v0

--- a/solution.py
+++ b/solution.py
@@ -78,7 +78,9 @@
         squares = lax.psum(jnp.sum(product * product, axis=1), "tensor")
         normed_z = (product * lax.rsqrt(squares / width + 1e-06)[:, None]).astype(jnp.bfloat16)
         partial_value = jnp.dot(normed_z, w_out[layer], preferred_element_type=jnp.float32)
-        state = state + lax.psum(partial_value.astype(jnp.bfloat16), "tensor").astype(jnp.float32)
+        state = state + jnp.sum(
+            lax.all_gather(partial_value.astype(jnp.bfloat16), "tensor"), axis=0
+        ).astype(jnp.float32)
         if layer + 1 < LAYERS:
             normed = row_norm(state).astype(jnp.bfloat16)
     return state[None]

time: 411 us -> 390 us (0.949)
  waiting for transfers between devices: 225 us -> 200 us
    psum x2 -> x0, waiting for transfers between devices: 42.8 us -> none  [on_device(): lax.psum(partial_value.astype(jnp.bfloat16), 'tensor').astype(jnp.float32)]
    all_gather x0 -> x2, waiting for transfers between devices: none -> 19 us  [on_device(): lax.all_gather(partial_value.astype(jnp.bfloat16), 'tensor')]
    reduce_sum x0 -> x2, other arithmetic: none -> 4.31 us  [on_device(): jnp.sum(lax.all_gather(partial_value.astype(jnp.bfloat16), 'tensor'), axi...]
  transfers between devices with their start and end apart: 6 -> 6, of which waited for: 6 -> 6; matrix products, arithmetic and copies ran while one was open for 13% -> 14% of each run, Pallas kernels for 0% -> 0%
where the time goes in v1:
time: 390 us; the launch traced here: 389 us
  waiting for transfers between devices  200 us (51%)
  matrix products  65.4 us (17%)
  local copies, waits for them, and re-layouts  61.5 us (16%)
  blocking collectives  26.5 us (7%)
  other arithmetic  20.9 us (5%)
  between operations  14.3 us (4%)
    all_gather x2, waiting for transfers between devices, on_device(): lax.all_gather(hist_values[0, layer], ('cand', 'tensor'), axis=0, tiled=T...  125 us
    all_gather x2, waiting for transfers between devices, on_device(): lax.all_gather(hist_keys[0, layer], ('cand', 'tensor'), axis=0, tiled=True)  56.2 us
    dot_general x8, matrix products, one_head(): return jnp.dot(weights, value_one, preferred_element_type=jnp.float32)  47.6 us
    all_gather x1, blocking collectives, on_device(): items = lax.all_gather(hist_ids[0], ('cand', 'tensor'), axis=0, tiled=True)  21.6 us
    all_gather x2, waiting for transfers between devices, on_device(): lax.all_gather(partial_value.astype(jnp.bfloat16), 'tensor')  19 us
    dynamic_slice x2, local copies, waits for them, and re-layouts, on_device(): values = lax.dynamic_slice_in_dim(values, column, local, 1)  18.8 us
    unnamed x20, local copies, waits for them, and re-layouts  11.9 us
    dot_general x2, matrix products, on_device(): jnp.dot(normed, w_in[layer].reshape(width, 4 * local), preferred_element_...  11.9 us
  transfers between devices with their start and end apart: 6, of which 6 were waited for; matrix products, arithmetic and copies ran while one was open for 14% of the time, Pallas kernels for 0%

profile of v1, /device:TPU:1, one launch (start us, length us, event | category | flops | bytes accessed | tf_op | source)
XLA Modules:
  0.0 388.9 jit_solution(12853186851614032077)
XLA Ops:
  11.8 7.0 %fusion.68 = (bf16[1,1024,4,512]{3,2,1,0:T(4,128)(2,1)}, bf16[1,1024,4,512]{3,2,1,0:T(4,128)(2,1)S(1)}) fusion(bf16[2,1024,4,512]{3,2,1,0:T(4,128)(2,1)} %param.22), kind=kLoop, calls=%fused_computation.82 | loop fusion | bytes 16777216 | tf_op jit(solution)/shard_map/slice | solution.py:30
  20.5 4.9 %divide_multiply_fusion.1 = f32[512,2048]{1,0:T(8,128)} fusion(bf16[1024,2048]{1,0:T(8,128)(2,1)S(1)} %bitcast.180, bf16[1,512,1024]{2,1,0:T(8,128)(2,1)S(1)} %copy-done, f32[512]{0:T(512)S(1)} %add_rsqrt_fusion.3), kind=kOutput, calls=%fused_computation.37 | convolution fusion | flops 2153250816 | bytes 9439232 | tf_op jit(solution)/shard_map/dot_general | solution.py:29
  25.4 5.4 %copy.25 = f32[512,2048]{0,1:T(8,128)} copy(f32[512,2048]{1,0:T(8,128)} %divide_multiply_fusion.1) | data formatting | bytes 8388608 | tf_op jit(solution)/shard_map/reshape | solution.py:33
  32.1 3.8 convert.19
  36.6 21.6 %all-gather.2 = s32[1,4096]{1,0:T(1,128)S(1)} all-gather(s32[1,256]{1,0:T(1,128)S(1)} %copy-done.5), channel_id=4, replica_groups=mesh['user'=8,'cand'=8,'tensor'=2] {'cand','tensor'}, dimensions={1}, use_global_device_ids=true | all-gather | bytes 17408 | tf_op jit(solution)/shard_map/all_gather | solution.py:42
  60.6 13.5 %all-gather.14.cloned.1.call-done = bf16[1,1,4096,1024]{2,3,1,0:T(8,128)(2,1)} async-done(((bf16[1,1,256,1024]{2,3,1,0:T(8,128)(2,1)}), bf16[1,1,4096,1024]{2,3,1,0:T(8,128)(2,1)}) %all-gather.14.cloned.1.call-update) | async-done | bytes 8388624 | tf_op jit(solution)/shard_map/all_gather | solution.py:40
  74.1 62.4 %all-gather.16.cloned.1.call-done = bf16[1,1,4096,1024]{2,3,1,0:T(8,128)(2,1)} async-done(((bf16[1,1,256,1024]{2,3,1,0:T(8,128)(2,1)}), bf16[1,1,4096,1024]{2,3,1,0:T(8,128)(2,1)}) %all-gather.16.cloned.1.call-update) | async-done | bytes 8388624 | tf_op jit(solution)/shard_map/all_gather | solution.py:41
  136.5 33.8 %conditional.2 = (f32[4,512,128]{2,1,0:T(8,128)}) conditional(s32[]{:T(128)} %convert_element_type.177, () %tuple.33, (bf16[4096,1024]{0,1:T(8,128)(2,1)}, s32[]{:T(128)}, bf16[4096,1024]{0,1:T(8,128)(2,1)}, s32[]{:T(128)}, s32[4096]{0:T(1024)S(1)}, /*index=5*/s32[1,512]{1,0:T(1,128)S(1)}, bf16[4,512,128]{1,2,0:T(8,128)(2,1)S(1)}) %tuple.106), branch_computations={%region_1.2_spmd, %region_2.5_spmd} | conditional | flops 1092620288 | bytes 19296452 | solution.py:64
  136.5 9.4 %constant_dynamic-slice_fusion = (bf16[4096,512]{0,1:T(8,128)(2,1)}, bf16[4096,512]{0,1:T(8,128)(2,1)}) fusion(bf16[4096,1024]{0,1:T(8,128)(2,1)} %get-tuple-element.174, s32[]{:T(128)} %get-tuple-element.170, bf16[4096,1024]{0,1:T(8,128)(2,1)} %get-tuple-element.169), kind=kLoop, calls=%fused_computation.17 | loop fusion | bytes 16777220 | tf_op jit(solution)/shard_map/dynamic_slice | solution.py:45
  146.6 23.7 %while.32 = (s32[]{:T(128)}, f32[4,512,128]{2,1,0:T(8,128)}, bf16[4,512,128]{1,2,0:T(8,128)(2,1)S(1)}, bf16[4,4096,128]{1,2,0:T(8,128)(2,1)}, bf16[4,4096,128]{1...) while((s32[]{:T(128)}, f32[4,512,128]{2,1,0:T(8,128)}, ...), condition=%wide.region_4.4_spmd.clone, body=%wide.region_3.3_spmd.clone.sunk | while | flops 1092616192 | bytes 2515045 | solution.py:62
  146.6 5.9 %fusion.92 = f32[4,512,128]{2,1,0:T(8,128)} fusion(f32[4,512,128]{2,1,0:T(8,128)} %get-tuple-element.446, s32[]{:T(128)S(6)} %copy.49, s32[4096]{0:T(1024)S(1)} %get-tuple-element.460, s32[512]{0:T(512)S(1)} %get-tuple-element.459, pred[4096]{0:T(1024)(128)(4,1)S(1)} %get-tuple-element.461, bf16[4,4096,128]{1,2,0:T(8,128)(2,1)} %get-tuple-element.458, ...), kind=kOutput, calls=%fused_computation.5.clone.1 | convolution fusion | flops 1092616192 | bytes 2514944 | tf_op jit(solution)/shard_map/cond/branch_1_fun/while/body/eval_jaxpr/dot_general | solution.py:60
  152.6 5.9 %fusion.92 = f32[4,512,128]{2,1,0:T(8,128)} fusion(f32[4,512,128]{2,1,0:T(8,128)} %get-tuple-element.446, s32[]{:T(128)S(6)} %copy.49, s32[4096]{0:T(1024)S(1)} %get-tuple-element.460, s32[512]{0:T(512)S(1)} %get-tuple-element.459, pred[4096]{0:T(1024)(128)(4,1)S(1)} %get-tuple-element.461, bf16[4,4096,128]{1,2,0:T(8,128)(2,1)} %get-tuple-element.458, ...), kind=kOutput, calls=%fused_computation.5.clone.1 | convolution fusion | flops 1092616192 | bytes 2514944 | tf_op jit(solution)/shard_map/cond/branch_1_fun/while/body/eval_jaxpr/dot_general | solution.py:60
  158.5 5.9 %fusion.92 = f32[4,512,128]{2,1,0:T(8,128)} fusion(f32[4,512,128]{2,1,0:T(8,128)} %get-tuple-element.446, s32[]{:T(128)S(6)} %copy.49, s32[4096]{0:T(1024)S(1)} %get-tuple-element.460, s32[512]{0:T(512)S(1)} %get-tuple-element.459, pred[4096]{0:T(1024)(128)(4,1)S(1)} %get-tuple-element.461, bf16[4,4096,128]{1,2,0:T(8,128)(2,1)} %get-tuple-element.458, ...), kind=kOutput, calls=%fused_computation.5.clone.1 | convolution fusion | flops 1092616192 | bytes 2514944 | tf_op jit(solution)/shard_map/cond/branch_1_fun/while/body/eval_jaxpr/dot_general | solution.py:60
  164.4 5.9 %fusion.92 = f32[4,512,128]{2,1,0:T(8,128)} fusion(f32[4,512,128]{2,1,0:T(8,128)} %get-tuple-element.446, s32[]{:T(128)S(6)} %copy.49, s32[4096]{0:T(1024)S(1)} %get-tuple-element.460, s32[512]{0:T(512)S(1)} %get-tuple-element.459, pred[4096]{0:T(1024)(128)(4,1)S(1)} %get-tuple-element.461, bf16[4,4096,128]{1,2,0:T(8,128)(2,1)} %get-tuple-element.458, ...), kind=kOutput, calls=%fused_computation.5.clone.1 | convolution fusion | flops 1092616192 | bytes 2514944 | tf_op jit(solution)/shard_map/cond/branch_1_fun/while/body/eval_jaxpr/dot_general | solution.py:60
  177.1 3.0 convolution_convert_fusion.1
  182.6 5.6 %copy.38 = bf16[128,8,4,512]{3,1,2,0:T(8,128)(2,1)} copy(bf16[128,8,4,512]{3,2,1,0:T(4,128)(2,1)} %bitcast.165) | data formatting | bytes 8388608
  188.2 5.5 %all-gather.18.cloned.1.call-done = bf16[1024,1024]{1,0:T(8,128)(2,1)} async-done(((bf16[512,1024]{1,0:T(8,128)(2,1)}), bf16[1024,1024]{1,0:T(8,128)(2,1)}) %all-gather.18.cloned.1.call-update) | async-done | bytes 2097168 | tf_op jit(solution)/shard_map/all_gather | solution.py:82
  196.2 7.0 %divide_multiply_fusion = f32[512,2048]{1,0:T(8,128)} fusion(bf16[1024,2048]{1,0:T(8,128)(2,1)} %bitcast.179, bf16[512,1024]{1,0:T(8,128)(2,1)S(1)} %reduce_sum.81, bf16[1,512,1024]{2,1,0:T(8,128)(2,1)S(1)} %copy-done, f32[512]{0:T(512)S(1)} %add_rsqrt_fusion.1), kind=kOutput, calls=%fused_computation.36 | convolution fusion | flops 2154299392 | bytes 10487808 | tf_op jit(solution)/shard_map/dot_general | solution.py:29
  203.2 5.4 %copy.26 = f32[512,2048]{0,1:T(8,128)} copy(f32[512,2048]{1,0:T(8,128)} %divide_multiply_fusion) | data formatting | bytes 8388608 | tf_op jit(solution)/shard_map/reshape | solution.py:33
  214.3 42.8 %all-gather.20.cloned.1.call-done = bf16[1,1,4096,1024]{2,3,1,0:T(8,128)(2,1)} async-done(((bf16[1,1,256,1024]{2,3,1,0:T(8,128)(2,1)}), bf16[1,1,4096,1024]{2,3,1,0:T(8,128)(2,1)}) %all-gather.20.cloned.1.call-update) | async-done | bytes 8388624 | tf_op jit(solution)/shard_map/all_gather | solution.py:40
  257.1 62.1 %all-gather.22.cloned.1.call-done = bf16[1,1,4096,1024]{2,3,1,0:T(8,128)(2,1)} async-done(((bf16[1,1,256,1024]{2,3,1,0:T(8,128)(2,1)}), bf16[1,1,4096,1024]{2,3,1,0:T(8,128)(2,1)}) %all-gather.22.cloned.1.call-update) | async-done | bytes 8388624 | tf_op jit(solution)/shard_map/all_gather | solution.py:41
  319.2 33.9 %conditional.3 = (f32[4,512,128]{2,1,0:T(8,128)}) conditional(s32[]{:T(128)} %convert_element_type.177, () %tuple.35, (bf16[4096,1024]{0,1:T(8,128)(2,1)}, s32[]{:T(128)}, bf16[4096,1024]{0,1:T(8,128)(2,1)}, s32[]{:T(128)}, s32[4096]{0:T(1024)S(1)}, /*index=5*/s32[1,512]{1,0:T(1,128)S(1)}, bf16[4,512,128]{1,2,0:T(8,128)(2,1)}) %tuple.107), branch_computations={%region_10.11_spmd, %region_11.14_spmd} | conditional | flops 1092620288 | bytes 19296452 | solution.py:64
  319.2 9.4 %constant_dynamic-slice_fusion.2 = (bf16[4096,512]{0,1:T(8,128)(2,1)}, bf16[4096,512]{0,1:T(8,128)(2,1)}) fusion(bf16[4096,1024]{0,1:T(8,128)(2,1)} %get-tuple-element.189, s32[]{:T(128)} %get-tuple-element.185, bf16[4096,1024]{0,1:T(8,128)(2,1)} %get-tuple-element.184), kind=kLoop, calls=%fused_computation.34 | loop fusion | bytes 16777220 | tf_op jit(solution)/shard_map/dynamic_slice | solution.py:45
  329.3 23.9 %while.33 = (s32[]{:T(128)}, f32[4,512,128]{2,1,0:T(8,128)}, bf16[4,512,128]{1,2,0:T(8,128)(2,1)}, bf16[4,4096,128]{1,2,0:T(8,128)(2,1)}, bf16[4,4096,128]{1,2,0...) while((s32[]{:T(128)}, f32[4,512,128]{2,1,0:T(8,128)}, ...), condition=%wide.region_13.13_spmd.clone, body=%wide.region_12.12_spmd.clone.sunk | while | flops 1092616192 | bytes 2515045 | solution.py:62
  329.3 6.0 %fusion.88 = f32[4,512,128]{2,1,0:T(8,128)} fusion(f32[4,512,128]{2,1,0:T(8,128)} %get-tuple-element.419, s32[]{:T(128)S(6)} %copy.42, s32[4096]{0:T(1024)S(1)} %get-tuple-element.433, s32[512]{0:T(512)S(1)} %get-tuple-element.432, pred[4096]{0:T(1024)(128)(4,1)S(1)} %get-tuple-element.434, bf16[4,4096,128]{1,2,0:T(8,128)(2,1)} %get-tuple-element.431, ...), kind=kOutput, calls=%fused_computation.22.clone.1 | convolution fusion | flops 1092616192 | bytes 2514944 | tf_op jit(solution)/shard_map/cond/branch_1_fun/while/body/eval_jaxpr/dot_general | solution.py:60
  335.3 6.0 %fusion.88 = f32[4,512,128]{2,1,0:T(8,128)} fusion(f32[4,512,128]{2,1,0:T(8,128)} %get-tuple-element.419, s32[]{:T(128)S(6)} %copy.42, s32[4096]{0:T(1024)S(1)} %get-tuple-element.433, s32[512]{0:T(512)S(1)} %get-tuple-element.432, pred[4096]{0:T(1024)(128)(4,1)S(1)} %get-tuple-element.434, bf16[4,4096,128]{1,2,0:T(8,128)(2,1)} %get-tuple-element.431, ...), kind=kOutput, calls=%fused_computation.22.clone.1 | convolution fusion | flops 1092616192 | bytes 2514944 | tf_op jit(solution)/shard_map/cond/branch_1_fun/while/body/eval_jaxpr/dot_general | solution.py:60
  341.3 6.0 %fusion.88 = f32[4,512,128]{2,1,0:T(8,128)} fusion(f32[4,512,128]{2,1,0:T(8,128)} %get-tuple-element.419, s32[]{:T(128)S(6)} %copy.42, s32[4096]{0:T(1024)S(1)} %get-tuple-element.433, s32[512]{0:T(512)S(1)} %get-tuple-element.432, pred[4096]{0:T(1024)(128)(4,1)S(1)} %get-tuple-element.434, bf16[4,4096,128]{1,2,0:T(8,128)(2,1)} %get-tuple-element.431, ...), kind=kOutput, calls=%fused_computation.22.clone.1 | convolution fusion | flops 1092616192 | bytes 2514944 | tf_op jit(solution)/shard_map/cond/branch_1_fun/while/body/eval_jaxpr/dot_general | solution.py:60
  347.2 6.0 %fusion.88 = f32[4,512,128]{2,1,0:T(8,128)} fusion(f32[4,512,128]{2,1,0:T(8,128)} %get-tuple-element.419, s32[]{:T(128)S(6)} %copy.42, s32[4096]{0:T(1024)S(1)} %get-tuple-element.433, s32[512]{0:T(512)S(1)} %get-tuple-element.432, pred[4096]{0:T(1024)(128)(4,1)S(1)} %get-tuple-element.434, bf16[4,4096,128]{1,2,0:T(8,128)(2,1)} %get-tuple-element.431, ...), kind=kOutput, calls=%fused_computation.22.clone.1 | convolution fusion | flops 1092616192 | bytes 2514944 | tf_op jit(solution)/shard_map/cond/branch_1_fun/while/body/eval_jaxpr/dot_general | solution.py:60
  353.2 2.5 copy.23
  357.3 2.5 psum.15
  361.5 2.9 convolution_convert_fusion
  364.5 13.5 %all-gather.24.cloned.1.call-done = bf16[1024,1024]{1,0:T(8,128)(2,1)} async-done(((bf16[512,1024]{1,0:T(8,128)(2,1)}), bf16[1024,1024]{1,0:T(8,128)(2,1)}) %all-gather.24.cloned.1.call-update) | async-done | bytes 2097168 | tf_op jit(solution)/shard_map/all_gather | solution.py:82
  (61 shorter events, 36.8 us)
Async XLA Ops:
  6.5 3.2 copy-start.4
  6.5 67.5 %all-gather.14.cloned.1.call-start = ((), (), s32[]{:S(2)}) async-start(), calls=%async_computation | async-start | bytes 8912896 | tf_op jit(solution)/shard_map/all_gather | solution.py:40
  9.7 126.8 %all-gather.16.cloned.1.call-start = ((), (), s32[]{:S(2)}) async-start(), calls=%async_computation.1 | async-start | bytes 8912896 | tf_op jit(solution)/shard_map/all_gather | solution.py:41
  11.7 181.9 %all-gather.18.cloned.1.call-start = ((), (), s32[]{:S(2)}) async-start(), calls=%async_computation.2 | async-start | bytes 3145728 | tf_op jit(solution)/shard_map/all_gather | solution.py:82
  18.8 1.4 copy-start
  30.7 5.8 %copy-start.5 = (s32[1,256]{1,0:T(1,128)S(1)}, s32[1,256]{1,0:T(1,128)}, u32[]{:S(2)}) copy-start(s32[1,256]{1,0:T(1,128)} %param.18) | copy-start | bytes 3076
  32.1 104.5 %copy-start.6 = (s32[1,512]{1,0:T(1,128)S(1)}, s32[1,512]{1,0:T(1,128)}, u32[]{:S(2)}) copy-start(s32[1,512]{1,0:T(1,128)} %param.17) | copy-start | bytes 6148
  177.1 3.1 copy-start.1
  177.1 4.2 %copy-start.2 = (bf16[1,1,256,1024]{3,2,1,0:T(8,128)(2,1)S(1)}, bf16[1,1,256,1024]{3,2,1,0:T(8,128)(2,1)}, u32[]{:S(2)}) copy-start(bf16[1,1,256,1024]{3,2,1,0:T(8,128)(2,1)} %get-tuple-element.307) | copy-start | bytes 1572868
  180.1 77.0 %all-gather.20.cloned.1.call-start = ((), (), s32[]{:S(2)}) async-start(), calls=%async_computation.3 | async-start | bytes 8912896 | tf_op jit(solution)/shard_map/all_gather | solution.py:40
  181.3 138.0 %all-gather.22.cloned.1.call-start = ((), (), s32[]{:S(2)}) async-start(), calls=%async_computation.4 | async-start | bytes 8912896 | tf_op jit(solution)/shard_map/all_gather | solution.py:41
  182.3 195.7 %all-gather.24.cloned.1.call-start = ((), (), s32[]{:S(2)}) async-start(), calls=%async_computation.5 | async-start | bytes 3145728 | tf_op jit(solution)/shard_map/all_gather | solution.py:82
  213.3 0.8 copy-start.3
Sparse Core Ops, SparseCore 0:
  9.8 64.1 all-gather.13
  75.7 60.7 all-gather.15
  180.3 13.3 all-gather.17
  195.1 61.9 all-gather.19
  258.6 60.6 all-gather.21
  364.6 13.3 all-gather.23
